TPU v7x, 32 devices: a whole 2x2x4 slice. The times are simulated.
32 devices in a mesh: seq: 8 (over z, x), fsdp: 4 (over y, core).
Axes of the slice: x: 2, y: 2, z: 4, core: 2. Of those that a mesh axis runs over, the one named last changes fastest.
Arguments:
- block_input: bfloat16 [8, 1024, 1536], P('fsdp', 'seq'), may hold values from -6 to 6
- dilated_weight: bfloat16 [3, 1536, 768], P(None, 'fsdp'), may hold values from -0.09375 to 0.09375
- w_project: bfloat16 [768, 1536], P('fsdp'), may hold values from -0.21875 to 0.21875
- gain_first: float32 [1536], replicated, may hold values from 0.5 to 1.5
- gain_second: float32 [768], replicated, may hold values from 0.5 to 1.5
- grad_output: bfloat16 [8, 1024, 1536], P('fsdp', 'seq'), may hold values from -6 to 6
Outputs:
- grad_input: bfloat16 [8, 1024, 1536], P('fsdp', 'seq')
- grad_gain_first: float32 [1536], replicated
- grad_gain_second: float32 [768], replicated
All inputs are finite; a program needn't handle non-finite values.
Results may differ from a plain program's by a relative error of at most 0.008.
Values may be sent and summed in bfloat16 or wider, within the bound.
A program may use at most 64 MiB of HBM per device.

v0:
```python
import jax
import jax.numpy as jnp
from jax import lax
from jax.sharding import PartitionSpec as P


def shifted(value, axis, steps):
    count = lax.axis_size(axis)
    initial, last = (max(0, -steps), min(count, count - steps))
    return lax.ppermute(value, axis, [(source, source + steps) for source in range(initial, last)])


def norm_act(values, factor):
    centre = values - jnp.mean(values, axis=-1, keepdims=True)
    spread = jnp.mean(centre * centre, axis=-1, keepdims=True)
    return jax.nn.gelu(centre * lax.rsqrt(spread + 1e-05) * factor)


def far_inputs(values, amount):
    return shifted(values, "seq", amount)


def far_grads(values, amount):
    return shifted(values, "seq", amount)


def three_taps(lagging, hidden_state, leading, w_full):
    mixed_state = jnp.einsum("sbc,ch->sbh", lagging, w_full[0], preferred_element_type=jnp.float32)
    mixed_state = mixed_state + jnp.einsum(
        "sbc,ch->sbh", hidden_state, w_full[1], preferred_element_type=jnp.float32
    )
    return mixed_state + jnp.einsum(
        "sbc,ch->sbh", leading, w_full[2], preferred_element_type=jnp.float32
    )


def block_grads(
    inputs, cotangent, w_full, proj_full, gain_first, gain_second, forward_mix, taps_grad
):
    widened = inputs.astype(jnp.float32)
    hidden_state = norm_act(widened, gain_first).astype(jnp.bfloat16)
    mixed_state = forward_mix(hidden_state).astype(jnp.bfloat16)
    grad_hidden2 = jnp.einsum(
        "sbc,hc->sbh", cotangent, proj_full, preferred_element_type=jnp.float32
    )
    unused, pull_second = jax.vjp(norm_act, mixed_state.astype(jnp.float32), gain_second)
    mixed_gradient, grad_second = pull_second(grad_hidden2)
    mixed_gradient = mixed_gradient.astype(jnp.bfloat16)
    grad_ahead, grad_behind = taps_grad(mixed_gradient)
    hidden_gradient = jnp.einsum(
        "sbh,ch->sbc", grad_ahead, w_full[0], preferred_element_type=jnp.float32
    )
    hidden_gradient = hidden_gradient + jnp.einsum(
        "sbh,ch->sbc", mixed_gradient, w_full[1], preferred_element_type=jnp.float32
    )
    hidden_gradient = hidden_gradient + jnp.einsum(
        "sbh,ch->sbc", grad_behind, w_full[2], preferred_element_type=jnp.float32
    )
    unused2, pull_first = jax.vjp(norm_act, widened, gain_first)
    grad_branch, grad_first = pull_first(hidden_gradient)
    grad_local = (cotangent.astype(jnp.float32) + grad_branch).astype(jnp.bfloat16)
    return (grad_local, grad_first, grad_second)


def body(block_input, dilated_weight, w_project, gain_first, gain_second, grad_output):
    w_full, proj_full = (
        lax.all_gather(dilated_weight, "fsdp", axis=1, tiled=True),
        lax.all_gather(w_project, "fsdp", axis=0, tiled=True),
    )
    reach = lax.axis_size("seq") // 8

    def remote_mix(hidden_state):
        return three_taps(
            far_inputs(hidden_state, reach), hidden_state, far_inputs(hidden_state, -reach), w_full
        )

    def remote_grads(values):
        return (far_grads(values, -reach), far_grads(values, reach))

    grad_input, first_sum, second_sum = block_grads(
        block_input,
        grad_output,
        w_full,
        proj_full,
        gain_first,
        gain_second,
        remote_mix,
        remote_grads,
    )
    totals = lax.psum((first_sum, second_sum), ("seq", "fsdp"))
    return (grad_input, totals[0], totals[1])


def solution(mesh):
    in_specs = (
        P("fsdp", "seq", None),
        P(None, "fsdp", None),
        P("fsdp", None),
        P(),
        P(),
        P("fsdp", "seq", None),
    )
    out_specs = (P("fsdp", "seq", None), P(), P())
    return jax.shard_map(body, mesh=mesh, in_specs=in_specs, out_specs=out_specs, check_vma=False)
```

profile of v0, /device:TPU:0, one launch (start us, length us, event | category | flops | bytes accessed | tf_op | source)
XLA Modules:
  0.0 168.9 jit_solution(13917864262040069713)
XLA Ops:
  7.2 0.0 copy-start
  7.2 0.0 copy-start.2
  7.2 0.0 all-gather.5.cloned.1.call-start
  7.2 0.7 all-gather.5.cloned.1.call-update
  7.9 0.0 all-gather.3.cloned.1.call-start
  8.0 0.7 all-gather.3.cloned.1.call-update
  8.7 0.0 copy-done
  8.7 0.2 convert_reduce_fusion
  8.9 0.3 fusion.23
  9.2 0.0 copy-done.2
  9.2 0.8 fusion.19
  10.0 1.3 collective-permute-start.1
  11.3 5.5 %collective-permute-start = (bf16[2,128,1536]{2,1,0:T(8,128)(2,1)S(1)}, bf16[2,128,1536]{2,1,0:T(8,128)(2,1)S(1)}, u32[]{:S(2)}, u32[]{:S(2)}) collective-permute-start(bf16[2,128,1536]{2,1,0:T(8,128)(2,1)S(1)} %fusion.19), channel_id=1, source_target_pairs={{0,4},{4,8},{8,12},{12,16},{16,20},{20,24},{24,28},{1,5},{5,9},{9,... | collective-permute-start | bytes 2359304 | tf_op jit(solution)/shard_map/ppermute | solution.py:10
  16.9 46.3 %all-gather.5.cloned.1.call-done = bf16[3,1536,768]{2,1,0:T(8,128)(2,1)} async-done(((bf16[3,384,768]{2,1,0:T(8,128)(2,1)}), bf16[3,1536,768]{2,1,0:T(8,128)(2,1)}) %all-gather.5.cloned.1.call-update) | async-done | bytes 7077904 | tf_op jit(solution)/shard_map/all_gather | solution.py:67
  63.2 2.4 %fusion.5 = f32[2,128,768]{2,1,0:T(8,128)S(1)} fusion(bf16[2,128,1536]{2,1,0:T(8,128)(2,1)S(1)} %fusion.19, bf16[3,1536,768]{2,1,0:T(8,128)(2,1)} %all-gather.5.cloned.1.call-done), kind=kOutput, calls=%fused_computation.12 | convolution fusion | flops 603979776 | bytes 3932160 | tf_op jit(solution)/shard_map/sbc,ch->sbh/dot_general | solution.py:29
  65.6 0.0 collective-permute-done.1
  65.6 2.4 %fusion.7 = f32[2,128,768]{2,1,0:T(8,128)S(1)} fusion(bf16[2,128,1536]{2,1,0:T(8,128)(2,1)S(1)} %collective-permute-done.1, bf16[3,1536,768]{2,1,0:T(8,128)(2,1)} %all-gather.5.cloned.1.call-done), kind=kOutput, calls=%fused_computation.14 | convolution fusion | flops 603979776 | bytes 3932160 | tf_op jit(solution)/shard_map/sbc,ch->sbh/dot_general | solution.py:32
  68.1 0.0 copy-start.1
  68.1 0.0 copy-start.3
  68.1 0.0 collective-permute-done
  68.1 2.6 %fusion.44 = (f32[2,128]{1,0:T(2,128)S(1)}, f32[2,128,768]{2,1,0:T(8,128)S(1)}) fusion(f32[2,128,768]{2,1,0:T(8,128)S(1)} %fusion.7, f32[2,128,768]{2,1,0:T(8,128)S(1)} %fusion.5, bf16[2,128,1536]{2,1,0:T(8,128)(2,1)S(1)} %collective-permute-done, bf16[3,1536,768]{2,1,0:T(8,128)(2,1)} %all-gather.5.cloned.1.call-done), kind=kOutput, calls=%fused_computation.67 | convolution fusion | flops 604962560 | bytes 5506048 | tf_op jit(solution)/shard_map/sbc,ch->sbh/dot_general | solution.py:28
  70.7 0.2 multiply_reduce_fusion.2
  70.9 17.9 %all-gather.3.cloned.1.call-done = bf16[768,1536]{1,0:T(8,128)(2,1)} async-done(((bf16[192,1536]{1,0:T(8,128)(2,1)}), bf16[768,1536]{1,0:T(8,128)(2,1)}) %all-gather.3.cloned.1.call-update) | async-done | bytes 2359312 | tf_op jit(solution)/shard_map/all_gather | solution.py:68
  88.8 0.0 copy-done.1
  88.8 0.0 copy-done.3
  88.8 3.0 %multiply_reduce_fusion.1 = (f32[2,128]{1,0:T(2,128)S(1)}, f32[2,128,768]{2,1,0:T(8,128)S(1)}) fusion(f32[2,128,768]{2,1,0:T(8,128)S(1)} %get-tuple-element.10, f32[768]{0:T(1024)S(1)} %copy-done.3, f32[2,128]{1,0:T(2,128)S(1)} %broadcast_multiply_fusion, f32[2,128]{1,0:T(2,128)S(1)} %fusion.43, bf16[2,128,1536]{2,1,0:T(8,128)(2,1)S(1)} %copy-done.1, ...), kind=kOutput, calls=%fused_computation.53 | convolution fusion | flops 608894720 | bytes 4724736 | tf_op jit(solution)/shard_map/sbc,hc->sbh/dot_general | solution.py:43
  91.8 0.5 multiply_reduce_fusion
  92.3 0.3 add_convert_fusion.1
  92.6 3.4 %collective-permute-start.3 = (bf16[2,128,768]{2,1,0:T(8,128)(2,1)S(1)}, bf16[2,128,768]{2,1,0:T(8,128)(2,1)S(1)}, u32[]{:S(2)}, u32[]{:S(2)}) collective-permute-start(bf16[2,128,768]{2,1,0:T(8,128)(2,1)S(1)} %add_convert_fusion.1), channel_id=1, source_target_pairs={{0,4},{4,8},{8,12},{12,16},{16,20},{20,24},{24,28},{1,5},{5,9},{9,... | collective-permute-start | bytes 1179656 | tf_op jit(solution)/shard_map/ppermute | solution.py:10
  96.0 1.3 collective-permute-start.2
  97.3 2.5 %fusion.4 = f32[2,128,1536]{2,1,0:T(8,128)S(1)} fusion(bf16[2,128,768]{2,1,0:T(8,128)(2,1)S(1)} %add_convert_fusion.1, bf16[3,1536,768]{2,1,0:T(8,128)(2,1)} %all-gather.5.cloned.1.call-done), kind=kOutput, calls=%fused_computation.11 | convolution fusion | flops 603979776 | bytes 4325376 | tf_op jit(solution)/shard_map/sbh,ch->sbc/dot_general | solution.py:53
  99.8 13.4 %collective-permute-done.3 = bf16[2,128,768]{2,1,0:T(8,128)(2,1)S(1)} collective-permute-done((bf16[2,128,768]{2,1,0:T(8,128)(2,1)S(1)}, bf16[2,128,768]{2,1,0:T(8,128)(2,1)S(1)}, u32[]{:S(2)}, u32[]{:S(2)}) %collective-permute-start.3) | collective-permute-done | bytes 393248 | tf_op jit(solution)/shard_map/ppermute | solution.py:10
  113.2 2.5 %fusion.6 = f32[2,128,1536]{2,1,0:T(8,128)S(1)} fusion(bf16[2,128,768]{2,1,0:T(8,128)(2,1)S(1)} %collective-permute-done.3, bf16[3,1536,768]{2,1,0:T(8,128)(2,1)} %all-gather.5.cloned.1.call-done), kind=kOutput, calls=%fused_computation.13 | convolution fusion | flops 603979776 | bytes 4325376 | tf_op jit(solution)/shard_map/sbh,ch->sbc/dot_general | solution.py:56
  115.6 0.0 collective-permute-done.2
  115.6 3.7 %fusion.24 = (f32[2,128]{1,0:T(2,128)S(1)}, f32[2,128,1536]{2,1,0:T(8,128)S(1)}) fusion(bf16[2,128,1536]{2,1,0:T(8,128)(2,1)S(1)} %copy-done, f32[1536]{0:T(1024)S(1)} %copy-done.2, f32[2,128]{1,0:T(2,128)S(1)} %broadcast_multiply_fusion.1, f32[2,128]{1,0:T(2,128)S(1)} %fusion.42, f32[2,128,1536]{2,1,0:T(8,128)S(1)} %fusion.6, ...), kind=kOutput, calls=%fused_computation.33 | convolution fusion | flops 614989568 | bytes 8266752 | tf_op jit(solution)/shard_map/sbh,ch->sbc/dot_general | solution.py:50
  119.4 0.7 fusion.22
  120.1 1.5 add_convert_fusion
  121.6 40.4 %all-reduce = (f32[1536]{0:T(1024)}, f32[768]{0:T(1024)}) all-reduce(f32[1536]{0:T(1024)S(1)} %get-tuple-element.3, f32[768]{0:T(1024)S(1)} %get-tuple-element.5), channel_id=1, replica_groups=mesh['seq'=8,'fsdp'=4] {'seq','fsdp'}, use_global_device_ids=true, to_apply=%region_9.0 | all-reduce | flops 2304 | bytes 18432 | tf_op jit(solution)/shard_map/psum | solution.py:90
  (8 shorter events, 0.1 us)
Async XLA Ops:
  7.2 1.5 copy-start
  7.2 2.1 %copy-start.2 = (f32[1536]{0:T(1024)S(1)}, f32[1536]{0:T(1024)}, u32[]{:S(2)}) copy-start(f32[1536]{0:T(1024)} %param.9) | copy-start | bytes 18436
  7.2 56.0 %all-gather.5.cloned.1.call-start = ((), (), s32[]{:S(2)}) async-start(), calls=%async_computation.1 | async-start | bytes 8847360 | tf_op jit(solution)/shard_map/all_gather | solution.py:67
  7.9 80.9 %all-gather.3.cloned.1.call-start = ((), (), s32[]{:S(2)}) async-start(), calls=%async_computation | async-start | bytes 2949120 | tf_op jit(solution)/shard_map/all_gather | solution.py:68
  10.0 55.6 %collective-permute-start.1 = (bf16[2,128,1536]{2,1,0:T(8,128)(2,1)S(1)}, bf16[2,128,1536]{2,1,0:T(8,128)(2,1)S(1)}, u32[]{:S(2)}, u32[]{:S(2)}) collective-permute-start(bf16[2,128,1536]{2,1,0:T(8,128)(2,1)S(1)} %fusion.19), channel_id=1, source_target_pairs={{4,0},{8,4},{12,8},{16,12},{20,16},{24,20},{28,24},{5,1},{9,5},{13... | collective-permute-start | bytes 2359304 | tf_op jit(solution)/shard_map/ppermute | solution.py:10
  11.3 56.8 %collective-permute-start = (bf16[2,128,1536]{2,1,0:T(8,128)(2,1)S(1)}, bf16[2,128,1536]{2,1,0:T(8,128)(2,1)S(1)}, u32[]{:S(2)}, u32[]{:S(2)}) collective-permute-start(bf16[2,128,1536]{2,1,0:T(8,128)(2,1)S(1)} %fusion.19), channel_id=1, source_target_pairs={{0,4},{4,8},{8,12},{12,16},{16,20},{20,24},{24,28},{1,5},{5,9},{9,... | collective-permute-start | bytes 2359304 | tf_op jit(solution)/shard_map/ppermute | solution.py:10
  68.1 20.8 %copy-start.1 = (bf16[2,128,1536]{2,1,0:T(8,128)(2,1)S(1)}, bf16[2,128,1536]{2,1,0:T(8,128)(2,1)}, u32[]{:S(2)}) copy-start(bf16[2,128,1536]{2,1,0:T(8,128)(2,1)} %param.11) | copy-start | bytes 2359300
  68.1 20.8 %copy-start.3 = (f32[768]{0:T(1024)S(1)}, f32[768]{0:T(1024)}, u32[]{:S(2)}) copy-start(f32[768]{0:T(1024)} %param.10) | copy-start | bytes 9220
  92.6 20.6 %collective-permute-start.3 = (bf16[2,128,768]{2,1,0:T(8,128)(2,1)S(1)}, bf16[2,128,768]{2,1,0:T(8,128)(2,1)S(1)}, u32[]{:S(2)}, u32[]{:S(2)}) collective-permute-start(bf16[2,128,768]{2,1,0:T(8,128)(2,1)S(1)} %add_convert_fusion.1), channel_id=1, source_target_pairs={{0,4},{4,8},{8,12},{12,16},{16,20},{20,24},{24,28},{1,5},{5,9},{9,... | collective-permute-start | bytes 1179656 | tf_op jit(solution)/shard_map/ppermute | solution.py:10
  96.0 19.7 %collective-permute-start.2 = (bf16[2,128,768]{2,1,0:T(8,128)(2,1)S(1)}, bf16[2,128,768]{2,1,0:T(8,128)(2,1)S(1)}, u32[]{:S(2)}, u32[]{:S(2)}) collective-permute-start(bf16[2,128,768]{2,1,0:T(8,128)(2,1)S(1)} %add_convert_fusion.1), channel_id=1, source_target_pairs={{4,0},{8,4},{12,8},{16,12},{20,16},{24,20},{28,24},{5,1},{9,5},{13... | collective-permute-start | bytes 1179656 | tf_op jit(solution)/shard_map/ppermute | solution.py:10
Sparse Core Ops, SparseCore 0:
  9.6 53.5 all-gather.4
  64.7 24.0 all-gather.2
where the time goes:
time: 169 us
  waiting for transfers between devices  79 us (47%)
  blocking collectives  40.4 us (24%)
  matrix products  19.1 us (11%)
  between operations  14.2 us (8%)
  starting transfers between devices  11.6 us (7%)
  other arithmetic  4.61 us (3%)
    all_gather x1, waiting for transfers between devices, body(): lax.all_gather(dilated_weight, 'fsdp', axis=1, tiled=True)  46.3 us
    psum x1, blocking collectives, body(): totals = lax.psum((first_sum, second_sum), ('seq', 'fsdp'))  40.4 us
    all_gather x1, waiting for transfers between devices, body(): lax.all_gather(w_project, 'fsdp', axis=0, tiled=True)  17.9 us
    ppermute x4, waiting for transfers between devices, shifted(): lax.ppermute(value, axis, [(source, source + steps) for source in range(i...  13.4 us
    ppermute x4, starting transfers between devices, shifted(): lax.ppermute(value, axis, [(source, source + steps) for source in range(i...  11.5 us
    dot_general x1, matrix products, block_grads(): jnp.einsum('sbh,ch->sbc', grad_ahead, w_full[0], preferred_element_type=j...  3.72 us
  transfers between devices with their start and end apart: 6, of which 3 were waited for; matrix products, arithmetic and copies ran while one was open for 8% of the time, Pallas kernels for 0%

commit v1 on v0

v1 whole, which is shorter than its diff:
```python
import functools

import jax
import jax.numpy as jnp
from jax import lax
from jax.experimental import pallas as pl
from jax.experimental.pallas import tpu as pltpu
from jax.sharding import PartitionSpec as P

MESH = pl.DeviceIdType.MESH
TAPS = (0, 2, 1)
CHUNKS = 2
UNITS = 4
EPS = 1e-05
K0 = 0.7978845608028654
K1 = 0.044715


def normed(values):
    centre = values - jnp.mean(values, axis=-1, keepdims=True)
    scale = lax.rsqrt(jnp.mean(centre * centre, axis=-1, keepdims=True) + EPS)
    return centre * scale, scale


def gelu_parts(a):
    square = a * a
    t = jnp.tanh(a * (K0 + (K0 * K1) * square))
    half = 0.5 + 0.5 * t
    slope = half + (0.5 * a) * (1.0 - t * t) * (K0 + (3.0 * K0 * K1) * square)
    return a * half, slope


def dot(a, b):
    return jnp.dot(a, b, preferred_element_type=jnp.float32)


def dot_t(a, b):
    return lax.dot_general(a, b, (((1,), (1,)), ((), ())), preferred_element_type=jnp.float32)


def fold(values):
    rows, columns = values.shape
    return jnp.sum(values.reshape(rows // 8, 8, columns), axis=0)


def kernel(
    seqs, x_ref, w_ref, p_ref, g1_ref, g2_ref, go_ref,
    out_ref, sum1_ref, sum2_ref,
    xbuf, gbuf, wbuf, pbuf, hbuf, n1, q1, r1, acc, n2, q2, r2, psend, rfwd, gmx, gh, obuf,
    part1, part2, fslots, sslots,
    y_s, y_r, z_s, z_r, a_s, a_r, b_s, b_r, own_s, own_r, own_l,
    sw_s, sw_r, sw_l, fw_s, fw_r, bw_s, bw_r, o_s, o_r, o_l, gf_s, gf_r, gs_s, gs_r,
):
    bins, chans = xbuf.shape[1], xbuf.shape[2]
    hid = pbuf.shape[0]
    wrows, prows = w_ref.shape[1], p_ref.shape[0]
    s, f = lax.axis_index("seq"), lax.axis_index("fsdp")
    reach = seqs // 8
    block = s // reach
    p, q = block // 2, block % 2
    zp = p % 2
    mate = s + reach - 2 * reach * q
    zmate = s + 2 * reach - 4 * reach * zp
    nxt, prv = s + 2 * reach, s - 2 * reach
    sib = f + 1 - 2 * (f % 2)
    far = (f + 2) % 4
    far_sib = (sib + 2) % 4

    def rc(src, dst, ss, rs, seq, fs):
        return pltpu.make_async_remote_copy(
            src_ref=src, dst_ref=dst, send_sem=ss, recv_sem=rs,
            device_id=(seq, fs), device_id_type=MESH,
        )

    barrier = pltpu.get_barrier_semaphore()

    def greet(i, carry):
        pl.semaphore_signal(barrier, inc=1, device_id=((s + i) % seqs, f), device_id_type=MESH)
        return carry

    lax.fori_loop(1, seqs, greet, 0)
    for i in range(1, 4):
        pl.semaphore_signal(barrier, inc=1, device_id=(s, (f + i) % 4), device_id_type=MESH)
    pl.semaphore_wait(barrier, seqs - 1 + 3)

    def held(u, owner, half, c):
        if u < 3:
            n = wrows // 2 // CHUNKS
            at = pl.multiple_of(owner * wrows + half * (wrows // 2) + c * n, 16)
            return wbuf.at[TAPS[u], pl.ds(at, n)]
        n = prows // 2 // CHUNKS
        at = pl.multiple_of(owner * prows + half * (prows // 2) + c * n, 16)
        return pbuf.at[pl.ds(at, n)]

    def mine(u, half, c):
        if u < 3:
            n = wrows // 2 // CHUNKS
            return w_ref.at[TAPS[u], pl.ds(pl.multiple_of(half * (wrows // 2) + c * n, 16), n)]
        n = prows // 2 // CHUNKS
        return p_ref.at[pl.ds(pl.multiple_of(half * (prows // 2) + c * n, 16), n)]

    def held_unit(u, owner):
        if u < 3:
            return wbuf.at[TAPS[u], pl.ds(pl.multiple_of(owner * wrows, 16), wrows)]
        return pbuf.at[pl.ds(pl.multiple_of(owner * prows, 16), prows)]

    def my_unit(u):
        return w_ref.at[TAPS[u]] if u < 3 else p_ref

    def y_copy(j, owner):
        u, c = j // CHUNKS, j % CHUNKS
        return rc(mine(u, zp, c), held(u, owner, zp, c), y_s.at[j], y_r.at[j], s, far)

    def z_copy(j, half):
        piece = held(j // CHUNKS, far, half, j % CHUNKS)
        return rc(piece, piece, z_s.at[j], z_r.at[j], zmate, f)

    def a_copy(j, owner):
        piece = held(j // CHUNKS, owner, zp, j % CHUNKS)
        return rc(piece, piece, a_s.at[j], a_r.at[j], s, sib)

    def b_copy(j, owner):
        piece = held(j // CHUNKS, owner, 1 - zp, j % CHUNKS)
        return rc(piece, piece, b_s.at[j], b_r.at[j], s, sib)

    def own_copy(u, owner):
        return rc(my_unit(u), held_unit(u, owner), own_s.at[u], own_r.at[u], s, sib)

    def own_local(u):
        return pltpu.make_async_copy(my_unit(u), held_unit(u, f), own_l.at[u])

    def swap(k, slot):
        ref, buf = ((x_ref, xbuf), (go_ref, gbuf))[k]
        return rc(ref.at[1 - q], buf.at[slot], sw_s.at[k], sw_r.at[k], mate, f)

    def swap_local(k):
        ref, buf = ((x_ref, xbuf), (go_ref, gbuf))[k]
        return pltpu.make_async_copy(ref.at[q], buf.at[q], sw_l.at[k])

    steps = UNITS * CHUNKS
    swap_local(0).start()
    swap(0, q).start()
    for j in range(steps):
        y_copy(j, f).start()
    for u in range(UNITS):
        own_copy(u, f).start()
        own_local(u).start()
    swap(1, q).start()
    swap_local(1).start()

    tile = 32
    per = bins // tile

    def first_act(which):
        def go(i, carry):
            at = pl.multiple_of(which * bins + i * tile, tile)
            rows = pl.ds(at, tile)
            v = xbuf[which, pl.ds(pl.multiple_of(i * tile, tile), tile), :].astype(jnp.float32)
            n, scale = normed(v)
            act, slope = gelu_parts(n * g1_ref[...])
            hbuf[rows, :] = act.astype(jnp.bfloat16)
            n1[rows, :] = n
            q1[rows, :] = slope
            r1[rows, :] = jnp.broadcast_to(scale, (tile, 128))
            return carry

        lax.fori_loop(0, per, go, 0)

    def pump(j):
        if j < steps:
            y_copy(j, far).wait_recv()
            z_copy(j, zp).start()
            a_copy(j, far).start()
        if 0 < j <= steps:
            z_copy(j - 1, 1 - zp).wait_recv()
            b_copy(j - 1, far).start()

    def unit_ready(u):
        own_local(u).wait()
        own_copy(u, sib).wait_recv()
        for c in range(CHUNKS):
            a_copy(u * CHUNKS + c, far_sib).wait_recv()
            b_copy(u * CHUNKS + c, far_sib).wait_recv()

    swap_local(0).wait()
    first_act(q)
    pump(0)
    pump(1)
    swap(0, 1 - q).wait_recv()
    first_act(1 - q)
    pump(2)
    unit_ready(0)

    def fwd(k):
        return dot(hbuf[...], wbuf[k])

    tap = fwd(0)
    acc[bins:, :] = tap[:bins, :]
    psend[0] = tap[bins:, :].astype(jnp.bfloat16)
    last = seqs // (2 * reach) - 1

    def to_next(src, dst, ss, rs):
        return rc(src, dst, ss, rs, nxt, f)

    def to_prev(src, dst, ss, rs):
        return rc(src, dst, ss, rs, prv, f)

    fwd_next = to_next(psend.at[0], rfwd.at[0], fw_s.at[0], fw_r.at[0])
    fwd_prev = to_prev(psend.at[1], rfwd.at[1], fw_s.at[1], fw_r.at[1])
    pl.when(p < last)(lambda: fwd_next.start())
    pump(3)
    pump(4)
    unit_ready(1)
    tap = fwd(2)
    acc[:bins, :] = tap[bins:, :]
    psend[1] = tap[:bins, :].astype(jnp.bfloat16)
    pl.when(p > 0)(lambda: fwd_prev.start())
    pump(5)
    pump(6)
    unit_ready(2)
    acc[...] += fwd(1)
    pump(7)

    def zero_first():
        rfwd[0] = jnp.zeros_like(rfwd[0])
        gmx[:bins, :] = jnp.zeros((bins, hid), jnp.bfloat16)

    def zero_last():
        rfwd[1] = jnp.zeros_like(rfwd[1])
        gmx[3 * bins:, :] = jnp.zeros((bins, hid), jnp.bfloat16)

    pl.when(p == 0)(zero_first)
    pl.when(p == last)(zero_last)
    pl.when(p > 0)(lambda: fwd_next.wait_recv())
    pl.when(p < last)(lambda: fwd_prev.wait_recv())

    def second_act(i, carry):
        for which in range(2):
            rows = pl.ds(pl.multiple_of(which * bins + i * tile, tile), tile)
            got = rfwd[which, pl.ds(pl.multiple_of(i * tile, tile), tile), :]
            v = (acc[rows, :] + got.astype(jnp.float32)).astype(jnp.bfloat16).astype(jnp.float32)
            n, scale = normed(v)
            unused, slope = gelu_parts(n * g2_ref[...])
            n2[rows, :] = n
            q2[rows, :] = slope
            r2[rows, :] = jnp.broadcast_to(scale, (tile, 128))
        return carry

    lax.fori_loop(0, per, second_act, 0)
    pump(8)
    swap_local(1).wait()
    swap(1, 1 - q).wait_recv()
    unit_ready(3)
    acc[...] = dot_t(gbuf[...].reshape(2 * bins, chans), pbuf[...])

    def back(rows, d, n, slope, r, gain, part):
        da = d * slope
        part[...] += fold(da * n)
        dn = da * gain
        m1 = jnp.mean(dn, axis=-1, keepdims=True)
        m2 = jnp.mean(dn * n, axis=-1, keepdims=True)
        return r[rows, 0:1] * (dn - m1 - n * m2)

    part1[...] = jnp.zeros_like(part1)
    part2[...] = jnp.zeros_like(part2)

    def second_back(i, carry):
        rows = pl.ds(pl.multiple_of(i * tile, tile), tile)
        dv = back(rows, acc[rows, :], n2[rows, :], q2[rows, :], r2, g2_ref[...], part2)
        gmx[pl.ds(pl.multiple_of(bins + i * tile, tile), tile), :] = dv.astype(jnp.bfloat16)
        return carry

    lax.fori_loop(0, 2 * per, second_back, 0)

    bwd_next = to_next(gmx.at[pl.ds(2 * bins, bins)], gmx.at[pl.ds(0, bins)], bw_s.at[0], bw_r.at[0])
    bwd_prev = to_prev(gmx.at[pl.ds(bins, bins)], gmx.at[pl.ds(3 * bins, bins)], bw_s.at[1], bw_r.at[1])
    pl.when(p < last)(lambda: bwd_next.start())
    pl.when(p > 0)(lambda: bwd_prev.start())
    gh[...] = dot_t(gmx[bins:3 * bins, :], wbuf[1])
    pl.when(p > 0)(lambda: bwd_next.wait_recv())
    pl.when(p < last)(lambda: bwd_prev.wait_recv())
    gh[...] += dot_t(gmx[2 * bins:, :], wbuf[0])
    gh[...] += dot_t(gmx[:2 * bins, :], wbuf[2])

    def first_back(which):
        def go(i, carry):
            rows = pl.ds(pl.multiple_of(which * bins + i * tile, tile), tile)
            here = pl.ds(pl.multiple_of(i * tile, tile), tile)
            dv = back(rows, gh[rows, :], n1[rows, :], q1[rows, :], r1, g1_ref[...], part1)
            obuf[which, here, :] = (gbuf[which, here, :].astype(jnp.float32) + dv).astype(jnp.bfloat16)
            return carry

        lax.fori_loop(0, per, go, 0)

    first_back(1 - q)
    out_mate = rc(obuf.at[1 - q], out_ref.at[q], o_s.at[0], o_r.at[0], mate, f)
    out_mate.start()
    first_back(q)
    out_own = pltpu.make_async_copy(obuf.at[q], out_ref.at[q], o_l.at[0])
    out_own.start()

    fslots[f, :, :chans] = jnp.sum(part1[...], axis=0, keepdims=True)
    fslots[f, :, chans:] = jnp.sum(part2[...], axis=0, keepdims=True)

    def f_copy(owner, other):
        return rc(fslots.at[owner], fslots.at[owner], gf_s.at[other], gf_r.at[owner], s, other)

    for i in range(1, 4):
        f_copy(f, (f + i) % 4).start()
    for i in range(1, 4):
        f_copy((f + i) % 4, (f + i) % 4).wait_recv()
    sslots[s] = jnp.sum(fslots[...], axis=0)

    def s_copy(owner, other):
        return rc(sslots.at[owner], sslots.at[owner], gs_s.at[other], gs_r.at[owner], other, f)

    def s_send(i, carry):
        s_copy(s, (s + i) % seqs).start()
        return carry

    def s_recv(i, carry):
        s_copy((s + i) % seqs, (s + i) % seqs).wait_recv()
        return carry

    def s_done(i, carry):
        s_copy(s, (s + i) % seqs).wait_send()
        return carry

    lax.fori_loop(1, seqs, s_send, 0)
    lax.fori_loop(1, seqs, s_recv, 0)
    total = jnp.sum(sslots[...], axis=0)
    sum1_ref[...] = total[:, :chans]
    sum2_ref[...] = total[:, chans:]

    lax.fori_loop(1, seqs, s_done, 0)
    for i in range(1, 4):
        f_copy(f, (f + i) % 4).wait_send()
    for j in range(steps):
        y_copy(j, f).wait_send()
        z_copy(j, zp).wait_send()
        a_copy(j, far).wait_send()
        b_copy(j, far).wait_send()
    for u in range(UNITS):
        own_copy(u, f).wait_send()
    for k in range(2):
        swap(k, q).wait_send()
    pl.when(p < last)(lambda: fwd_next.wait_send())
    pl.when(p > 0)(lambda: fwd_prev.wait_send())
    pl.when(p < last)(lambda: bwd_next.wait_send())
    pl.when(p > 0)(lambda: bwd_prev.wait_send())
    out_own.wait()
    out_mate.wait_send()
    rc(obuf.at[1 - q], out_ref.at[1 - q], o_s.at[0], o_r.at[0], mate, f).wait_recv()


def body(block_input, dilated_weight, w_project, gain_first, gain_second, grad_output):
    seqs = lax.axis_size("seq")
    fsdps = lax.axis_size("fsdp")
    samples, bins, chans = block_input.shape
    hid = w_project.shape[0] * fsdps
    rows = 2 * bins
    bf16, f32 = jnp.bfloat16, jnp.float32
    dma = lambda n: pltpu.SemaphoreType.DMA((n,))
    steps = UNITS * CHUNKS
    anywhere = pl.BlockSpec(memory_space=pl.ANY)
    vmem = pl.BlockSpec(memory_space=pltpu.VMEM)
    out, sum1, sum2 = pl.pallas_call(
        functools.partial(kernel, seqs),
        out_shape=(
            jax.ShapeDtypeStruct(block_input.shape, bf16),
            jax.ShapeDtypeStruct((1, chans), f32),
            jax.ShapeDtypeStruct((1, hid), f32),
        ),
        in_specs=[anywhere, anywhere, anywhere, vmem, vmem, anywhere],
        out_specs=(anywhere, vmem, vmem),
        scratch_shapes=[
            pltpu.VMEM((2, bins, chans), bf16),
            pltpu.VMEM((2, bins, chans), bf16),
            pltpu.VMEM((3, chans, hid), bf16),
            pltpu.VMEM((hid, chans), bf16),
            pltpu.VMEM((rows, chans), bf16),
            pltpu.VMEM((rows, chans), f32),
            pltpu.VMEM((rows, chans), f32),
            pltpu.VMEM((rows, 128), f32),
            pltpu.VMEM((rows, hid), f32),
            pltpu.VMEM((rows, hid), f32),
            pltpu.VMEM((rows, hid), f32),
            pltpu.VMEM((rows, 128), f32),
            pltpu.VMEM((2, bins, hid), bf16),
            pltpu.VMEM((2, bins, hid), bf16),
            pltpu.VMEM((2 * rows, hid), bf16),
            pltpu.VMEM((rows, chans), f32),
            pltpu.VMEM((2, bins, chans), bf16),
            pltpu.VMEM((8, chans), f32),
            pltpu.VMEM((8, hid), f32),
            pltpu.VMEM((fsdps, 1, chans + hid), f32),
            pltpu.VMEM((seqs, 1, chans + hid), f32),
        ]
        + [dma(steps)] * 8
        + [dma(UNITS)] * 3
        + [dma(2)] * 3
        + [dma(2)] * 4
        + [dma(1)] * 3
        + [dma(fsdps)] * 2
        + [dma(seqs)] * 2,
        compiler_params=pltpu.CompilerParams(
            collective_id=0, has_side_effects=True, vmem_limit_bytes=52 * 1024 * 1024
        ),
    )(
        block_input, dilated_weight, w_project,
        gain_first.reshape(1, chans), gain_second.reshape(1, hid), grad_output,
    )
    return out, sum1.reshape(chans), sum2.reshape(hid)


def solution(mesh):
    in_specs = (
        P("fsdp", "seq", None),
        P(None, "fsdp", None),
        P("fsdp", None),
        P(),
        P(),
        P("fsdp", "seq", None),
    )
    out_specs = (P("fsdp", "seq", None), P(), P())
    return jax.shard_map(body, mesh=mesh, in_specs=in_specs, out_specs=out_specs, check_vma=False)
```

time: 169 us -> 78.1 us (0.46)
  waiting for transfers between devices: 79 us -> 0 us
  Pallas kernels: 0 us -> 72.7 us
  blocking collectives: 40.4 us -> 0 us
  matrix products: 19.1 us -> 0 us
  between operations: 14.2 us -> 0.64 us
  starting transfers between devices: 11.6 us -> 0 us
  other arithmetic: 4.61 us -> 1.22 us
  local copies, waits for them, and re-layouts: 0.02 us -> 3.33 us
    pallas_call x0 -> x1, Pallas kernels: none -> 72.7 us  [body(): pl.pallas_call(functools.partial(kernel, seqs), out_shape=(jax.ShapeDtype...]
    all_gather x2 -> x0, waiting for transfers between devices: 64.2 us -> none  [the longest x1 46.3 us: body(): lax.all_gather(dilated_weight, 'fsdp', axis=1, tiled=True)]
    psum x1 -> x0, blocking collectives: 40.4 us -> none  [body(): totals = lax.psum((first_sum, second_sum), ('seq', 'fsdp'))]
    dot_general x7 -> x0, matrix products: 19.1 us -> none  [the longest x1 3.72 us: block_grads(): jnp.einsum('sbh,ch->sbc', grad_ahead, w_full[0], preferred_element_type=j...]
    ppermute x4 -> x0, waiting for transfers between devices: 13.4 us -> none  [shifted(): lax.ppermute(value, axis, [(source, source + steps) for source in range(i...]
    ppermute x4 -> x0, starting transfers between devices: 11.5 us -> none  [shifted(): lax.ppermute(value, axis, [(source, source + steps) for source in range(i...]
    convert_element_type x3 -> x0, other arithmetic: 2.58 us -> none  [the longest x1 1.52 us: block_grads(): (cotangent.astype(jnp.float32) + grad_branch).astype(jnp.bfloat16)]
    reduce_sum x5 -> x0, other arithmetic: 1.96 us -> none  [the longest x2 1.2 us: norm_act(): return jax.nn.gelu(centre * lax.rsqrt(spread + 1e-05) * factor)]
  transfers between devices with their start and end apart: 6 -> 0, of which waited for: 3 -> 0; matrix products, arithmetic and copies ran while one was open for 8% -> 0% of each run, Pallas kernels for 0% -> 0%
where the time goes in v1:
time: 78.1 us; the launch traced here: 77.9 us
  Pallas kernels  72.7 us (93%)
  local copies, waits for them, and re-layouts  3.33 us (4%)
  other arithmetic  1.22 us (2%)
    pallas_call x1, Pallas kernels, body(): pl.pallas_call(functools.partial(kernel, seqs), out_shape=(jax.ShapeDtype...  72.7 us
    unnamed x3, local copies, waits for them, and re-layouts  1.94 us

profile of v1, /device:TPU:0, one launch (start us, length us, event | category | flops | bytes accessed | tf_op | source)
XLA Modules:
  0.0 77.9 jit_solution(16188366402994875103)
XLA Ops:
  0.6 0.7 reshape.19.g2_ref
  1.3 0.7 reshape.18.g1_ref
  2.0 0.0 copy-start
  2.0 1.1 %copy-done = bf16[192,1536]{1,0:T(8,128)(2,1)S(1)} copy-done((bf16[192,1536]{1,0:T(8,128)(2,1)S(1)}, bf16[192,1536]{1,0:T(8,128)(2,1)}, u32[]{:S(2)}) %copy-start) | copy-done | bytes 589848
  3.1 72.7 %shard_map.85 = (bf16[2,128,1536]{2,1,0:T(8,128)(2,1)S(1)}, f32[1,1536]{1,0:T(1,128)S(1)}, f32[1,768]{1,0:T(1,128)S(1)}) custom-call(bf16[2,128,1536]{2,1,0:T(8,128)(2,1)} %x_ref.1, bf16[3,384,768]{2,1,0:T(8,128)(2,1)} %w_ref.1, bf16[192,1536]{1,0:T(8,128)(2,1)S(1)} %copy-done, f32[1,1536]{1,0:T(1,128)S(1)} %reshape.18.g1_ref, f32[1,768]{1,0:T(1,128)S(1)} %reshape.19.g2_ref, ...), custom_call_target="tpu_custom_call" | custom-call | tf_op jit(solution)/shard_map/pallas_call | solution.py:367
  75.8 0.6 reduce.1
  76.4 0.6 reduce
  77.0 0.9 %copy.10 = bf16[2,128,1536]{2,1,0:T(8,128)(2,1)} copy(bf16[2,128,1536]{2,1,0:T(8,128)(2,1)S(1)} %get-tuple-element.12) | data formatting | bytes 1572864
Async XLA Ops:
  2.0 1.1 %copy-start = (bf16[192,1536]{1,0:T(8,128)(2,1)S(1)}, bf16[192,1536]{1,0:T(8,128)(2,1)}, u32[]{:S(2)}) copy-start(bf16[192,1536]{1,0:T(8,128)(2,1)} %p_ref.1) | copy-start | bytes 1769476

commit v2 on v1

--- a/solution.py
+++ b/solution.py
@@ -9,7 +9,9 @@
 
 MESH = pl.DeviceIdType.MESH
 TAPS = (0, 2, 1)
-CHUNKS = 2
+CHUNKS = 3
+LAG = 2
+AHEAD = 3
 UNITS = 4
 EPS = 1e-05
 K0 = 0.7978845608028654
@@ -107,20 +109,32 @@
     def my_unit(u):
         return w_ref.at[TAPS[u]] if u < 3 else p_ref
 
+    def route(j):
+        if j >= CHUNKS and j % CHUNKS == CHUNKS - 1:
+            return q, mate
+        return zp, zmate
+
     def y_copy(j, owner):
         u, c = j // CHUNKS, j % CHUNKS
-        return rc(mine(u, zp, c), held(u, owner, zp, c), y_s.at[j], y_r.at[j], s, far)
-
-    def z_copy(j, half):
+        half, unused = route(j)
+        return rc(mine(u, half, c), held(u, owner, half, c), y_s.at[j], y_r.at[j], s, far)
+
+    def z_send(j):
+        half, partner = route(j)
         piece = held(j // CHUNKS, far, half, j % CHUNKS)
-        return rc(piece, piece, z_s.at[j], z_r.at[j], zmate, f)
+        return rc(piece, piece, z_s.at[j], z_r.at[j], partner, f)
+
+    def z_recv(j):
+        half, partner = route(j)
+        piece = held(j // CHUNKS, far, 1 - half, j % CHUNKS)
+        return rc(piece, piece, z_s.at[j], z_r.at[j], partner, f)
 
     def a_copy(j, owner):
-        piece = held(j // CHUNKS, owner, zp, j % CHUNKS)
+        piece = held(j // CHUNKS, owner, route(j)[0], j % CHUNKS)
         return rc(piece, piece, a_s.at[j], a_r.at[j], s, sib)
 
     def b_copy(j, owner):
-        piece = held(j // CHUNKS, owner, 1 - zp, j % CHUNKS)
+        piece = held(j // CHUNKS, owner, 1 - route(j)[0], j % CHUNKS)
         return rc(piece, piece, b_s.at[j], b_r.at[j], s, sib)
 
     def own_copy(u, owner):
@@ -130,8 +144,10 @@
         return pltpu.make_async_copy(my_unit(u), held_unit(u, f), own_l.at[u])
 
     def swap(k, slot):
-        ref, buf = ((x_ref, xbuf), (go_ref, gbuf))[k]
-        return rc(ref.at[1 - q], buf.at[slot], sw_s.at[k], sw_r.at[k], mate, f)
+        if k == 0:
+            return rc(x_ref.at[1 - q], xbuf.at[slot], sw_s.at[0], sw_r.at[0], mate, f)
+        rows = pl.ds((k - 1) * (bins // 2), bins // 2)
+        return rc(go_ref.at[1 - q, rows], gbuf.at[slot, rows], sw_s.at[k], sw_r.at[k], mate, f)
 
     def swap_local(k):
         ref, buf = ((x_ref, xbuf), (go_ref, gbuf))[k]
@@ -140,12 +156,11 @@
     steps = UNITS * CHUNKS
     swap_local(0).start()
     swap(0, q).start()
-    for j in range(steps):
+    for j in range(AHEAD):
         y_copy(j, f).start()
     for u in range(UNITS):
         own_copy(u, f).start()
         own_local(u).start()
-    swap(1, q).start()
     swap_local(1).start()
 
     tile = 32
@@ -169,11 +184,13 @@
     def pump(j):
         if j < steps:
             y_copy(j, far).wait_recv()
-            z_copy(j, zp).start()
+            z_send(j).start()
+            if j + AHEAD < steps:
+                y_copy(j + AHEAD, f).start()
             a_copy(j, far).start()
-        if 0 < j <= steps:
-            z_copy(j - 1, 1 - zp).wait_recv()
-            b_copy(j - 1, far).start()
+        if j >= LAG:
+            z_recv(j - LAG).wait_recv()
+            b_copy(j - LAG, far).start()
 
     def unit_ready(u):
         own_local(u).wait()
@@ -189,7 +206,10 @@
     swap(0, 1 - q).wait_recv()
     first_act(1 - q)
     pump(2)
+    pump(3)
+    pump(4)
     unit_ready(0)
+    swap(1, q).start()
 
     def fwd(k):
         return dot(hbuf[...], wbuf[k])
@@ -208,18 +228,21 @@
     fwd_next = to_next(psend.at[0], rfwd.at[0], fw_s.at[0], fw_r.at[0])
     fwd_prev = to_prev(psend.at[1], rfwd.at[1], fw_s.at[1], fw_r.at[1])
     pl.when(p < last)(lambda: fwd_next.start())
-    pump(3)
-    pump(4)
+    pump(5)
+    pump(6)
+    pump(7)
     unit_ready(1)
+    swap(2, q).start()
     tap = fwd(2)
     acc[:bins, :] = tap[bins:, :]
     psend[1] = tap[:bins, :].astype(jnp.bfloat16)
     pl.when(p > 0)(lambda: fwd_prev.start())
-    pump(5)
-    pump(6)
+    pump(8)
+    pump(9)
+    pump(10)
+    pump(11)
     unit_ready(2)
     acc[...] += fwd(1)
-    pump(7)
 
     def zero_first():
         rfwd[0] = jnp.zeros_like(rfwd[0])
@@ -247,9 +270,11 @@
         return carry
 
     lax.fori_loop(0, per, second_act, 0)
-    pump(8)
+    pump(12)
+    pump(13)
     swap_local(1).wait()
     swap(1, 1 - q).wait_recv()
+    swap(2, 1 - q).wait_recv()
     unit_ready(3)
     acc[...] = dot_t(gbuf[...].reshape(2 * bins, chans), pbuf[...])
 
@@ -264,17 +289,20 @@
     part1[...] = jnp.zeros_like(part1)
     part2[...] = jnp.zeros_like(part2)
 
-    def second_back(i, carry):
-        rows = pl.ds(pl.multiple_of(i * tile, tile), tile)
-        dv = back(rows, acc[rows, :], n2[rows, :], q2[rows, :], r2, g2_ref[...], part2)
-        gmx[pl.ds(pl.multiple_of(bins + i * tile, tile), tile), :] = dv.astype(jnp.bfloat16)
-        return carry
-
-    lax.fori_loop(0, 2 * per, second_back, 0)
+    def second_back(which):
+        def go(i, carry):
+            rows = pl.ds(pl.multiple_of(which * bins + i * tile, tile), tile)
+            dv = back(rows, acc[rows, :], n2[rows, :], q2[rows, :], r2, g2_ref[...], part2)
+            gmx[pl.ds(pl.multiple_of(bins + which * bins + i * tile, tile), tile), :] = dv.astype(jnp.bfloat16)
+            return carry
+
+        lax.fori_loop(0, per, go, 0)
 
     bwd_next = to_next(gmx.at[pl.ds(2 * bins, bins)], gmx.at[pl.ds(0, bins)], bw_s.at[0], bw_r.at[0])
     bwd_prev = to_prev(gmx.at[pl.ds(bins, bins)], gmx.at[pl.ds(3 * bins, bins)], bw_s.at[1], bw_r.at[1])
+    second_back(1)
     pl.when(p < last)(lambda: bwd_next.start())
+    second_back(0)
     pl.when(p > 0)(lambda: bwd_prev.start())
     gh[...] = dot_t(gmx[bins:3 * bins, :], wbuf[1])
     pl.when(p > 0)(lambda: bwd_next.wait_recv())
@@ -282,20 +310,24 @@
     gh[...] += dot_t(gmx[2 * bins:, :], wbuf[0])
     gh[...] += dot_t(gmx[:2 * bins, :], wbuf[2])
 
-    def first_back(which):
+    def out_mate(i, which):
+        rows = pl.ds(pl.multiple_of(i * tile, tile), tile)
+        return rc(obuf.at[1 - q, rows], out_ref.at[which, rows], o_s.at[i], o_r.at[i], mate, f)
+
+    def first_back(which, send):
         def go(i, carry):
             rows = pl.ds(pl.multiple_of(which * bins + i * tile, tile), tile)
             here = pl.ds(pl.multiple_of(i * tile, tile), tile)
             dv = back(rows, gh[rows, :], n1[rows, :], q1[rows, :], r1, g1_ref[...], part1)
             obuf[which, here, :] = (gbuf[which, here, :].astype(jnp.float32) + dv).astype(jnp.bfloat16)
+            if send:
+                out_mate(i, q).start()
             return carry
 
         lax.fori_loop(0, per, go, 0)
 
-    first_back(1 - q)
-    out_mate = rc(obuf.at[1 - q], out_ref.at[q], o_s.at[0], o_r.at[0], mate, f)
-    out_mate.start()
-    first_back(q)
+    first_back(1 - q, True)
+    first_back(q, False)
     out_own = pltpu.make_async_copy(obuf.at[q], out_ref.at[q], o_l.at[0])
     out_own.start()
 
@@ -337,20 +369,21 @@
         f_copy(f, (f + i) % 4).wait_send()
     for j in range(steps):
         y_copy(j, f).wait_send()
-        z_copy(j, zp).wait_send()
+        z_send(j).wait_send()
         a_copy(j, far).wait_send()
         b_copy(j, far).wait_send()
     for u in range(UNITS):
         own_copy(u, f).wait_send()
-    for k in range(2):
+    for k in range(3):
         swap(k, q).wait_send()
     pl.when(p < last)(lambda: fwd_next.wait_send())
     pl.when(p > 0)(lambda: fwd_prev.wait_send())
     pl.when(p < last)(lambda: bwd_next.wait_send())
     pl.when(p > 0)(lambda: bwd_prev.wait_send())
     out_own.wait()
-    out_mate.wait_send()
-    rc(obuf.at[1 - q], out_ref.at[1 - q], o_s.at[0], o_r.at[0], mate, f).wait_recv()
+    for i in range(per):
+        out_mate(i, q).wait_send()
+        out_mate(i, 1 - q).wait_recv()
 
 
 def body(block_input, dilated_weight, w_project, gain_first, gain_second, grad_output):
@@ -398,13 +431,14 @@
         ]
         + [dma(steps)] * 8
         + [dma(UNITS)] * 3
-        + [dma(2)] * 3
-        + [dma(2)] * 4
-        + [dma(1)] * 3
+        + [dma(3)] * 2
+        + [dma(2)] * 5
+        + [dma(bins // 32)] * 2
+        + [dma(1)]
         + [dma(fsdps)] * 2
         + [dma(seqs)] * 2,
         compiler_params=pltpu.CompilerParams(
-            collective_id=0, has_side_effects=True, vmem_limit_bytes=52 * 1024 * 1024
+            collective_id=0, has_side_effects=True, vmem_limit_bytes=62 * 1024 * 1024
         ),
     )(
         block_input, dilated_weight, w_project,

time: 78.1 us -> 76.4 us (0.978)
  Pallas kernels: 72.7 us -> 68.1 us
  other arithmetic: 1.22 us -> 2.59 us
  local copies, waits for them, and re-layouts: 3.33 us -> 4.62 us
    pallas_call x1, Pallas kernels: 72.7 us -> 68.1 us  [body(): pl.pallas_call(functools.partial(kernel, seqs), out_shape=(jax.ShapeDtype...]
    pallas_call x2, other arithmetic: 1.22 us -> 2.59 us  [body(): pl.pallas_call(functools.partial(kernel, seqs), out_shape=(jax.ShapeDtype...]
    unnamed x3 -> x1, local copies, waits for them, and re-layouts: 1.94 us -> 2.06 us
where the time goes in v2:
time: 76.4 us; the launch traced here: 76 us
  Pallas kernels  68.1 us (89%)
  local copies, waits for them, and re-layouts  4.62 us (6%)
  other arithmetic  2.59 us (3%)
    pallas_call x1, Pallas kernels, body(): pl.pallas_call(functools.partial(kernel, seqs), out_shape=(jax.ShapeDtype...  68.1 us
    pallas_call x2, other arithmetic, body(): pl.pallas_call(functools.partial(kernel, seqs), out_shape=(jax.ShapeDtype...  2.59 us
    unnamed x1, local copies, waits for them, and re-layouts  2.06 us

profile of v2, /device:TPU:0, one launch (start us, length us, event | category | flops | bytes accessed | tf_op | source)
XLA Modules:
  0.0 76.0 jit_solution(13254129466981401499)
XLA Ops:
  0.6 1.3 %reshape.19.g2_ref = f32[1,768]{1,0:T(1,128)} reshape(f32[768]{0:T(1024)} %param.10) | data formatting | bytes 6144 | tf_op jit(solution)/shard_map/reshape | solution.py:445
  1.9 1.3 %reshape.18.g1_ref = f32[1,1536]{1,0:T(1,128)} reshape(f32[1536]{0:T(1024)} %param.9) | data formatting | bytes 12288 | tf_op jit(solution)/shard_map/reshape | solution.py:445
  3.2 68.1 %shard_map.85 = (bf16[2,128,1536]{2,1,0:T(8,128)(2,1)}, f32[1,1536]{1,0:T(1,128)}, f32[1,768]{1,0:T(1,128)}) custom-call(bf16[2,128,1536]{2,1,0:T(8,128)(2,1)} %x_ref.1, bf16[3,384,768]{2,1,0:T(8,128)(2,1)} %w_ref.1, bf16[192,1536]{1,0:T(8,128)(2,1)} %p_ref.1, f32[1,1536]{1,0:T(1,128)} %reshape.18.g1_ref, f32[1,768]{1,0:T(1,128)} %reshape.19.g2_ref, ...), custom_call_target="tpu_custom_call" | custom-call | tf_op jit(solution)/shard_map/pallas_call | solution.py:400
  71.3 1.3 %reduce.1 = f32[768]{0:T(1024)} reduce(f32[1,768]{1,0:T(1,128)} %get-tuple-element.8, f32[]{:T(128)} %constant.2), dimensions={0}, to_apply=%get-tuple-element.8.reduce_sub_computation | reduce | bytes 6148 | tf_op jit(solution)/shard_map/pallas_call | solution.py:400
  72.6 1.3 %reduce = f32[1536]{0:T(1024)} reduce(f32[1,1536]{1,0:T(1,128)} %get-tuple-element.7, f32[]{:T(128)} %constant.2), dimensions={0}, to_apply=%get-tuple-element.7.reduce_sub_computation | reduce | bytes 12292 | tf_op jit(solution)/shard_map/pallas_call | solution.py:400
  73.9 2.1 %copy.10 = bf16[2,128,1536]{2,1,0:T(8,128)(2,1)} copy(bf16[2,128,1536]{2,1,0:T(8,128)(2,1)} %get-tuple-element.12) | data formatting | bytes 1572864

commit v3 on v2

--- a/solution.py
+++ b/solution.py
@@ -48,7 +48,7 @@
 def kernel(
     seqs, x_ref, w_ref, p_ref, g1_ref, g2_ref, go_ref,
     out_ref, sum1_ref, sum2_ref,
-    xbuf, gbuf, wbuf, pbuf, hbuf, n1, q1, r1, acc, n2, q2, r2, psend, rfwd, gmx, gh, obuf,
+    xbuf, gbuf, wbuf, pbuf, hbuf, n1, q1, r1, acc, n2, q2, r2, psend, rfwd, gmx, gh, ght, g2t, obuf,
     part1, part2, fslots, sslots,
     y_s, y_r, z_s, z_r, a_s, a_r, b_s, b_r, own_s, own_r, own_l,
     sw_s, sw_r, sw_l, fw_s, fw_r, bw_s, bw_r, o_s, o_r, o_l, gf_s, gf_r, gs_s, gs_r,
@@ -192,12 +192,23 @@
             z_recv(j - LAG).wait_recv()
             b_copy(j - LAG, far).start()
 
-    def unit_ready(u):
+    def near_ready(u):
         own_local(u).wait()
         own_copy(u, sib).wait_recv()
+
+    def unit_ready(u):
         for c in range(CHUNKS):
             a_copy(u * CHUNKS + c, far_sib).wait_recv()
             b_copy(u * CHUNKS + c, far_sib).wait_recv()
+
+    side = f // 2
+
+    def span(which, size):
+        return pl.ds(pl.multiple_of(which * size, 128), size)
+
+    def fwd(k, which):
+        rows = span(which, 2 * wrows)
+        return dot(hbuf[:, rows], wbuf[k, rows, :])
 
     swap_local(0).wait()
     first_act(q)
@@ -206,17 +217,20 @@
     swap(0, 1 - q).wait_recv()
     first_act(1 - q)
     pump(2)
+    near_ready(0)
+    n2[...] = fwd(0, side)
     pump(3)
+    near_ready(1)
+    q2[...] = fwd(2, side)
     pump(4)
+    near_ready(2)
+    acc[...] = fwd(1, side)
     unit_ready(0)
     swap(1, q).start()
 
-    def fwd(k):
-        return dot(hbuf[...], wbuf[k])
-
-    tap = fwd(0)
-    acc[bins:, :] = tap[:bins, :]
-    psend[0] = tap[bins:, :].astype(jnp.bfloat16)
+    n2[...] += fwd(0, 1 - side)
+    acc[bins:, :] += n2[:bins, :]
+    psend[0] = n2[bins:, :].astype(jnp.bfloat16)
     last = seqs // (2 * reach) - 1
 
     def to_next(src, dst, ss, rs):
@@ -233,16 +247,16 @@
     pump(7)
     unit_ready(1)
     swap(2, q).start()
-    tap = fwd(2)
-    acc[:bins, :] = tap[bins:, :]
-    psend[1] = tap[:bins, :].astype(jnp.bfloat16)
+    q2[...] += fwd(2, 1 - side)
+    acc[:bins, :] += q2[bins:, :]
+    psend[1] = q2[:bins, :].astype(jnp.bfloat16)
     pl.when(p > 0)(lambda: fwd_prev.start())
     pump(8)
     pump(9)
     pump(10)
     pump(11)
     unit_ready(2)
-    acc[...] += fwd(1)
+    acc[...] += fwd(1, 1 - side)
 
     def zero_first():
         rfwd[0] = jnp.zeros_like(rfwd[0])
@@ -271,12 +285,19 @@
 
     lax.fori_loop(0, per, second_act, 0)
     pump(12)
-    pump(13)
     swap_local(1).wait()
     swap(1, 1 - q).wait_recv()
     swap(2, 1 - q).wait_recv()
+    near_ready(3)
+
+    def grad_hidden2(which):
+        rows = span(which, 2 * prows)
+        g2t[rows, :] = dot_t(pbuf[rows, :], gbuf[...].reshape(2 * bins, chans))
+
+    grad_hidden2(side)
+    pump(13)
     unit_ready(3)
-    acc[...] = dot_t(gbuf[...].reshape(2 * bins, chans), pbuf[...])
+    grad_hidden2(1 - side)
 
     def back(rows, d, n, slope, r, gain, part):
         da = d * slope
@@ -296,6 +317,7 @@
             gmx[pl.ds(pl.multiple_of(bins + which * bins + i * tile, tile), tile), :] = dv.astype(jnp.bfloat16)
             return carry
 
+        acc[which * bins:(which + 1) * bins, :] = g2t[:, which * bins:(which + 1) * bins].T
         lax.fori_loop(0, per, go, 0)
 
     bwd_next = to_next(gmx.at[pl.ds(2 * bins, bins)], gmx.at[pl.ds(0, bins)], bw_s.at[0], bw_r.at[0])
@@ -304,11 +326,13 @@
     pl.when(p < last)(lambda: bwd_next.start())
     second_back(0)
     pl.when(p > 0)(lambda: bwd_prev.start())
-    gh[...] = dot_t(gmx[bins:3 * bins, :], wbuf[1])
+    ght[...] = dot_t(wbuf[1], gmx[bins:3 * bins, :])
     pl.when(p > 0)(lambda: bwd_next.wait_recv())
     pl.when(p < last)(lambda: bwd_prev.wait_recv())
-    gh[...] += dot_t(gmx[2 * bins:, :], wbuf[0])
-    gh[...] += dot_t(gmx[:2 * bins, :], wbuf[2])
+    ght[...] += dot_t(wbuf[0], gmx[2 * bins:, :])
+    ght[...] += dot_t(wbuf[2], gmx[:2 * bins, :])
+    for i in range(2):
+        gh[i * bins:(i + 1) * bins, :] = ght[:, i * bins:(i + 1) * bins].T
 
     def out_mate(i, which):
         rows = pl.ds(pl.multiple_of(i * tile, tile), tile)
@@ -396,6 +420,7 @@
     dma = lambda n: pltpu.SemaphoreType.DMA((n,))
     steps = UNITS * CHUNKS
     anywhere = pl.BlockSpec(memory_space=pl.ANY)
+    hbm = pl.BlockSpec(memory_space=pltpu.HBM)
     vmem = pl.BlockSpec(memory_space=pltpu.VMEM)
     out, sum1, sum2 = pl.pallas_call(
         functools.partial(kernel, seqs),
@@ -404,7 +429,7 @@
             jax.ShapeDtypeStruct((1, chans), f32),
             jax.ShapeDtypeStruct((1, hid), f32),
         ),
-        in_specs=[anywhere, anywhere, anywhere, vmem, vmem, anywhere],
+        in_specs=[hbm, hbm, hbm, vmem, vmem, hbm],
         out_specs=(anywhere, vmem, vmem),
         scratch_shapes=[
             pltpu.VMEM((2, bins, chans), bf16),
@@ -423,6 +448,8 @@
             pltpu.VMEM((2, bins, hid), bf16),
             pltpu.VMEM((2 * rows, hid), bf16),
             pltpu.VMEM((rows, chans), f32),
+            pltpu.VMEM((chans, rows), f32),
+            pltpu.VMEM((hid, rows), f32),
             pltpu.VMEM((2, bins, chans), bf16),
             pltpu.VMEM((8, chans), f32),
             pltpu.VMEM((8, hid), f32),
@@ -438,7 +465,7 @@
         + [dma(fsdps)] * 2
         + [dma(seqs)] * 2,
         compiler_params=pltpu.CompilerParams(
-            collective_id=0, has_side_effects=True, vmem_limit_bytes=62 * 1024 * 1024
+            collective_id=0, has_side_effects=True, vmem_limit_bytes=52 * 1024 * 1024
         ),
     )(
         block_input, dilated_weight, w_project,

time: 76.4 us -> 74.1 us (0.970)
  other arithmetic: 2.59 us -> 1.22 us
  local copies, waits for them, and re-layouts: 4.62 us -> 3.33 us
    pallas_call x2, other arithmetic: 2.59 us -> 1.22 us  [body(): pl.pallas_call(functools.partial(kernel, seqs), out_shape=(jax.ShapeDtype...]
    unnamed x1 -> x3, local copies, waits for them, and re-layouts: 2.06 us -> 1.94 us
where the time goes in v3:
time: 74.1 us; the launch traced here: 73.8 us
  Pallas kernels  68.6 us (93%)
  local copies, waits for them, and re-layouts  3.33 us (4%)
  other arithmetic  1.22 us (2%)
    pallas_call x1, Pallas kernels, body(): pl.pallas_call(functools.partial(kernel, seqs), out_shape=(jax.ShapeDtype...  68.6 us
    unnamed x3, local copies, waits for them, and re-layouts  1.94 us

profile of v3, /device:TPU:0, one launch (start us, length us, event | category | flops | bytes accessed | tf_op | source)
XLA Modules:
  0.0 73.8 jit_solution(17638041909777690412)
XLA Ops:
  0.6 0.7 reshape.19.g2_ref
  1.3 0.7 reshape.18.g1_ref
  2.0 0.0 copy-start
  2.0 1.1 %copy-done = bf16[192,1536]{1,0:T(8,128)(2,1)S(1)} copy-done((bf16[192,1536]{1,0:T(8,128)(2,1)S(1)}, bf16[192,1536]{1,0:T(8,128)(2,1)}, u32[]{:S(2)}) %copy-start) | copy-done | bytes 589848
  3.1 68.6 %shard_map.85 = (bf16[2,128,1536]{2,1,0:T(8,128)(2,1)S(1)}, f32[1,1536]{1,0:T(1,128)S(1)}, f32[1,768]{1,0:T(1,128)S(1)}) custom-call(bf16[2,128,1536]{2,1,0:T(8,128)(2,1)} %x_ref.1, bf16[3,384,768]{2,1,0:T(8,128)(2,1)} %w_ref.1, bf16[192,1536]{1,0:T(8,128)(2,1)S(1)} %copy-done, f32[1,1536]{1,0:T(1,128)S(1)} %reshape.18.g1_ref, f32[1,768]{1,0:T(1,128)S(1)} %reshape.19.g2_ref, ...), custom_call_target="tpu_custom_call" | custom-call | tf_op jit(solution)/shard_map/pallas_call | solution.py:425
  71.7 0.6 reduce.1
  72.3 0.6 reduce
  72.9 0.9 %copy.10 = bf16[2,128,1536]{2,1,0:T(8,128)(2,1)} copy(bf16[2,128,1536]{2,1,0:T(8,128)(2,1)S(1)} %get-tuple-element.12) | data formatting | bytes 1572864
Async XLA Ops:
  2.0 1.1 %copy-start = (bf16[192,1536]{1,0:T(8,128)(2,1)S(1)}, bf16[192,1536]{1,0:T(8,128)(2,1)}, u32[]{:S(2)}) copy-start(bf16[192,1536]{1,0:T(8,128)(2,1)} %p_ref.1) | copy-start | bytes 1769476

commit v4 on v3

--- a/solution.py
+++ b/solution.py
@@ -9,9 +9,10 @@
 
 MESH = pl.DeviceIdType.MESH
 TAPS = (0, 2, 1)
+GROUPS = 2
 CHUNKS = 3
 LAG = 2
-AHEAD = 3
+AHEAD = 5
 UNITS = 4
 EPS = 1e-05
 K0 = 0.7978845608028654
@@ -258,13 +259,15 @@
     unit_ready(2)
     acc[...] += fwd(1, 1 - side)
 
+    part = bins // GROUPS
+
     def zero_first():
         rfwd[0] = jnp.zeros_like(rfwd[0])
-        gmx[:bins, :] = jnp.zeros((bins, hid), jnp.bfloat16)
+        gmx[:, :part, :] = jnp.zeros((GROUPS, part, hid), jnp.bfloat16)
 
     def zero_last():
         rfwd[1] = jnp.zeros_like(rfwd[1])
-        gmx[3 * bins:, :] = jnp.zeros((bins, hid), jnp.bfloat16)
+        gmx[:, 3 * part:, :] = jnp.zeros((GROUPS, part, hid), jnp.bfloat16)
 
     pl.when(p == 0)(zero_first)
     pl.when(p == last)(zero_last)
@@ -299,9 +302,9 @@
     unit_ready(3)
     grad_hidden2(1 - side)
 
-    def back(rows, d, n, slope, r, gain, part):
+    def back(rows, d, n, slope, r, gain, total):
         da = d * slope
-        part[...] += fold(da * n)
+        total[...] += fold(da * n)
         dn = da * gain
         m1 = jnp.mean(dn, axis=-1, keepdims=True)
         m2 = jnp.mean(dn * n, axis=-1, keepdims=True)
@@ -310,48 +313,62 @@
     part1[...] = jnp.zeros_like(part1)
     part2[...] = jnp.zeros_like(part2)
 
-    def second_back(which):
+    for i in range(2):
+        acc[i * bins:(i + 1) * bins, :] = g2t[:, i * bins:(i + 1) * bins].T
+    each = part // tile
+
+    def second_back(g, which):
         def go(i, carry):
-            rows = pl.ds(pl.multiple_of(which * bins + i * tile, tile), tile)
+            at = g * part + i * tile
+            rows = pl.ds(pl.multiple_of(which * bins + at, tile), tile)
             dv = back(rows, acc[rows, :], n2[rows, :], q2[rows, :], r2, g2_ref[...], part2)
-            gmx[pl.ds(pl.multiple_of(bins + which * bins + i * tile, tile), tile), :] = dv.astype(jnp.bfloat16)
+            to = pl.ds(pl.multiple_of((1 + which) * part + i * tile, tile), tile)
+            gmx[g, to, :] = dv.astype(jnp.bfloat16)
             return carry
 
-        acc[which * bins:(which + 1) * bins, :] = g2t[:, which * bins:(which + 1) * bins].T
-        lax.fori_loop(0, per, go, 0)
-
-    bwd_next = to_next(gmx.at[pl.ds(2 * bins, bins)], gmx.at[pl.ds(0, bins)], bw_s.at[0], bw_r.at[0])
-    bwd_prev = to_prev(gmx.at[pl.ds(bins, bins)], gmx.at[pl.ds(3 * bins, bins)], bw_s.at[1], bw_r.at[1])
-    second_back(1)
-    pl.when(p < last)(lambda: bwd_next.start())
-    second_back(0)
-    pl.when(p > 0)(lambda: bwd_prev.start())
-    ght[...] = dot_t(wbuf[1], gmx[bins:3 * bins, :])
-    pl.when(p > 0)(lambda: bwd_next.wait_recv())
-    pl.when(p < last)(lambda: bwd_prev.wait_recv())
-    ght[...] += dot_t(wbuf[0], gmx[2 * bins:, :])
-    ght[...] += dot_t(wbuf[2], gmx[:2 * bins, :])
-    for i in range(2):
-        gh[i * bins:(i + 1) * bins, :] = ght[:, i * bins:(i + 1) * bins].T
+        lax.fori_loop(0, each, go, 0)
+
+    def bwd_next(g):
+        src, dst = gmx.at[g, pl.ds(2 * part, part)], gmx.at[g, pl.ds(0, part)]
+        return to_next(src, dst, bw_s.at[2 * g], bw_r.at[2 * g])
+
+    def bwd_prev(g):
+        src, dst = gmx.at[g, pl.ds(part, part)], gmx.at[g, pl.ds(3 * part, part)]
+        return to_prev(src, dst, bw_s.at[2 * g + 1], bw_r.at[2 * g + 1])
+
+    for g in range(GROUPS):
+        second_back(g, 1)
+        pl.when(p < last)(lambda: bwd_next(g).start())
+        second_back(g, 0)
+        pl.when(p > 0)(lambda: bwd_prev(g).start())
 
     def out_mate(i, which):
         rows = pl.ds(pl.multiple_of(i * tile, tile), tile)
         return rc(obuf.at[1 - q, rows], out_ref.at[which, rows], o_s.at[i], o_r.at[i], mate, f)
 
-    def first_back(which, send):
+    def first_back(g, which, send):
         def go(i, carry):
-            rows = pl.ds(pl.multiple_of(which * bins + i * tile, tile), tile)
-            here = pl.ds(pl.multiple_of(i * tile, tile), tile)
-            dv = back(rows, gh[rows, :], n1[rows, :], q1[rows, :], r1, g1_ref[...], part1)
+            rows = pl.ds(pl.multiple_of(which * part + i * tile, tile), tile)
+            at = g * part + i * tile
+            all_rows = pl.ds(pl.multiple_of(which * bins + at, tile), tile)
+            here = pl.ds(pl.multiple_of(at, tile), tile)
+            dv = back(all_rows, gh[rows, :], n1[all_rows, :], q1[all_rows, :], r1, g1_ref[...], part1)
             obuf[which, here, :] = (gbuf[which, here, :].astype(jnp.float32) + dv).astype(jnp.bfloat16)
             if send:
-                out_mate(i, q).start()
+                out_mate(g * each + i, q).start()
             return carry
 
-        lax.fori_loop(0, per, go, 0)
-
-    first_back(1 - q, True)
-    first_back(q, False)
+        lax.fori_loop(0, each, go, 0)
+
+    for g in range(GROUPS):
+        ght[...] = dot_t(wbuf[1], gmx[g, part:3 * part, :])
+        pl.when(p > 0)(lambda: bwd_next(g).wait_recv())
+        pl.when(p < last)(lambda: bwd_prev(g).wait_recv())
+        ght[...] += dot_t(wbuf[0], gmx[g, 2 * part:, :])
+        ght[...] += dot_t(wbuf[2], gmx[g, :2 * part, :])
+        gh[...] = ght[...].T
+        first_back(g, 1 - q, True)
+        first_back(g, q, False)
     out_own = pltpu.make_async_copy(obuf.at[q], out_ref.at[q], o_l.at[0])
     out_own.start()
 
@@ -402,8 +419,9 @@
         swap(k, q).wait_send()
     pl.when(p < last)(lambda: fwd_next.wait_send())
     pl.when(p > 0)(lambda: fwd_prev.wait_send())
-    pl.when(p < last)(lambda: bwd_next.wait_send())
-    pl.when(p > 0)(lambda: bwd_prev.wait_send())
+    for g in range(GROUPS):
+        pl.when(p < last)(lambda: bwd_next(g).wait_send())
+        pl.when(p > 0)(lambda: bwd_prev(g).wait_send())
     out_own.wait()
     for i in range(per):
         out_mate(i, q).wait_send()
@@ -446,9 +464,9 @@
             pltpu.VMEM((rows, 128), f32),
             pltpu.VMEM((2, bins, hid), bf16),
             pltpu.VMEM((2, bins, hid), bf16),
-            pltpu.VMEM((2 * rows, hid), bf16),
-            pltpu.VMEM((rows, chans), f32),
-            pltpu.VMEM((chans, rows), f32),
+            pltpu.VMEM((GROUPS, 2 * rows // GROUPS, hid), bf16),
+            pltpu.VMEM((rows // GROUPS, chans), f32),
+            pltpu.VMEM((chans, rows // GROUPS), f32),
             pltpu.VMEM((hid, rows), f32),
             pltpu.VMEM((2, bins, chans), bf16),
             pltpu.VMEM((8, chans), f32),
@@ -459,7 +477,8 @@
         + [dma(steps)] * 8
         + [dma(UNITS)] * 3
         + [dma(3)] * 2
-        + [dma(2)] * 5
+        + [dma(2)] * 3
+        + [dma(2 * GROUPS)] * 2
         + [dma(bins // 32)] * 2
         + [dma(1)]
         + [dma(fsdps)] * 2

time: 74.1 us -> 73.8 us (level)
  no operation moved by 1% of the time
where the time goes in v4:
time: 73.8 us; the launch traced here: 73.6 us
  Pallas kernels  68.4 us (93%)
  local copies, waits for them, and re-layouts  3.33 us (5%)
  other arithmetic  1.22 us (2%)
    pallas_call x1, Pallas kernels, body(): pl.pallas_call(functools.partial(kernel, seqs), out_shape=(jax.ShapeDtype...  68.4 us
    unnamed x3, local copies, waits for them, and re-layouts  1.94 us

profile of v4, /device:TPU:0, one launch (start us, length us, event | category | flops | bytes accessed | tf_op | source)
XLA Modules:
  0.0 73.6 jit_solution(15205150485118838916)
XLA Ops:
  0.6 0.7 reshape.19.g2_ref
  1.3 0.7 reshape.18.g1_ref
  2.0 0.0 copy-start
  2.0 1.1 %copy-done = bf16[192,1536]{1,0:T(8,128)(2,1)S(1)} copy-done((bf16[192,1536]{1,0:T(8,128)(2,1)S(1)}, bf16[192,1536]{1,0:T(8,128)(2,1)}, u32[]{:S(2)}) %copy-start) | copy-done | bytes 589848
  3.1 68.4 %shard_map.85 = (bf16[2,128,1536]{2,1,0:T(8,128)(2,1)S(1)}, f32[1,1536]{1,0:T(1,128)S(1)}, f32[1,768]{1,0:T(1,128)S(1)}) custom-call(bf16[2,128,1536]{2,1,0:T(8,128)(2,1)} %x_ref.1, bf16[3,384,768]{2,1,0:T(8,128)(2,1)} %w_ref.1, bf16[192,1536]{1,0:T(8,128)(2,1)S(1)} %copy-done, f32[1,1536]{1,0:T(1,128)S(1)} %reshape.18.g1_ref, f32[1,768]{1,0:T(1,128)S(1)} %reshape.19.g2_ref, ...), custom_call_target="tpu_custom_call" | custom-call | tf_op jit(solution)/shard_map/pallas_call | solution.py:443
  71.5 0.6 reduce.1
  72.1 0.6 reduce
  72.7 0.9 %copy.10 = bf16[2,128,1536]{2,1,0:T(8,128)(2,1)} copy(bf16[2,128,1536]{2,1,0:T(8,128)(2,1)S(1)} %get-tuple-element.12) | data formatting | bytes 1572864
Async XLA Ops:
  2.0 1.1 %copy-start = (bf16[192,1536]{1,0:T(8,128)(2,1)S(1)}, bf16[192,1536]{1,0:T(8,128)(2,1)}, u32[]{:S(2)}) copy-start(bf16[192,1536]{1,0:T(8,128)(2,1)} %p_ref.1) | copy-start | bytes 1769476

commit v5 on v4

--- a/solution.py
+++ b/solution.py
@@ -215,15 +215,15 @@
     first_act(q)
     pump(0)
     pump(1)
+    pump(2)
+    pump(3)
     swap(0, 1 - q).wait_recv()
     first_act(1 - q)
-    pump(2)
+    pump(4)
     near_ready(0)
     n2[...] = fwd(0, side)
-    pump(3)
     near_ready(1)
     q2[...] = fwd(2, side)
-    pump(4)
     near_ready(2)
     acc[...] = fwd(1, side)
     unit_ready(0)

time: 73.8 us -> 70.5 us (0.955)
  Pallas kernels: 68.4 us -> 65 us
    pallas_call x1, Pallas kernels: 68.4 us -> 65 us  [body(): pl.pallas_call(functools.partial(kernel, seqs), out_shape=(jax.ShapeDtype...]
where the time goes in v5:
time: 70.5 us; the launch traced here: 70.2 us
  Pallas kernels  65 us (92%)
  local copies, waits for them, and re-layouts  3.33 us (5%)
  other arithmetic  1.22 us (2%)
    pallas_call x1, Pallas kernels, body(): pl.pallas_call(functools.partial(kernel, seqs), out_shape=(jax.ShapeDtype...  65 us
    unnamed x3, local copies, waits for them, and re-layouts  1.94 us

profile of v5, /device:TPU:0, one launch (start us, length us, event | category | flops | bytes accessed | tf_op | source)
XLA Modules:
  0.0 70.2 jit_solution(14332176531725547944)
XLA Ops:
  0.6 0.7 reshape.19.g2_ref
  1.3 0.7 reshape.18.g1_ref
  2.0 0.0 copy-start
  2.0 1.1 %copy-done = bf16[192,1536]{1,0:T(8,128)(2,1)S(1)} copy-done((bf16[192,1536]{1,0:T(8,128)(2,1)S(1)}, bf16[192,1536]{1,0:T(8,128)(2,1)}, u32[]{:S(2)}) %copy-start) | copy-done | bytes 589848
  3.1 65.0 %shard_map.85 = (bf16[2,128,1536]{2,1,0:T(8,128)(2,1)S(1)}, f32[1,1536]{1,0:T(1,128)S(1)}, f32[1,768]{1,0:T(1,128)S(1)}) custom-call(bf16[2,128,1536]{2,1,0:T(8,128)(2,1)} %x_ref.1, bf16[3,384,768]{2,1,0:T(8,128)(2,1)} %w_ref.1, bf16[192,1536]{1,0:T(8,128)(2,1)S(1)} %copy-done, f32[1,1536]{1,0:T(1,128)S(1)} %reshape.18.g1_ref, f32[1,768]{1,0:T(1,128)S(1)} %reshape.19.g2_ref, ...), custom_call_target="tpu_custom_call" | custom-call | tf_op jit(solution)/shard_map/pallas_call | solution.py:443
  68.1 0.6 reduce.1
  68.7 0.6 reduce
  69.4 0.9 %copy.10 = bf16[2,128,1536]{2,1,0:T(8,128)(2,1)} copy(bf16[2,128,1536]{2,1,0:T(8,128)(2,1)S(1)} %get-tuple-element.12) | data formatting | bytes 1572864
Async XLA Ops:
  2.0 1.1 %copy-start = (bf16[192,1536]{1,0:T(8,128)(2,1)S(1)}, bf16[192,1536]{1,0:T(8,128)(2,1)}, u32[]{:S(2)}) copy-start(bf16[192,1536]{1,0:T(8,128)(2,1)} %p_ref.1) | copy-start | bytes 1769476
